TPU v7x, 256 devices: a whole 4x4x8 slice. The times are simulated.
256 devices in a mesh: lon: 32 (over x_lo, z, core), lat: 8 (over x_hi, y).
Axes of the slice: x: 4 (x_hi: 2, x_lo: 2; x = x_hi * 2 + x_lo), y: 4, z: 8, core: 2. Of those that a mesh axis runs over, the one named last changes fastest.
Arguments:
- pixels: float32 [32, 32, 4096], P('lon', 'lat'), may hold values from -6 to 6
- patch_w: bfloat16 [32, 4, 1024], P('lon'), may hold values from -3 to 3
- var_embed: bfloat16 [32, 1024], replicated, may hold values from -6 to 6
- var_ids: int32 [32], replicated, may hold values from 0 to 31, each once
- agg_score: bfloat16 [1024, 16], replicated
- agg_value: bfloat16 [1024, 1024], replicated, may hold values from -0.1875 to 0.1875
- agg_out: bfloat16 [1024, 1024], replicated, may hold values from -0.1875 to 0.1875
- pos_embed: bfloat16 [16, 2048, 1024], P('lat', 'lon'), may hold values from -3 to 3
- norm_gain: float32 [1024], replicated, may hold values from 0.5 to 1.5
- w_query: bfloat16 [1024, 1024], replicated
- w_key: bfloat16 [1024, 1024], replicated
- w_value: bfloat16 [1024, 1024], replicated, may hold values from -0.1875 to 0.1875
- w_proj: bfloat16 [1024, 1024], replicated, may hold values from -0.1875 to 0.1875
- window_off: int32 [16], replicated, may hold values from -32 to 32
Outputs:
- updated: bfloat16 [16, 2048, 1024], P('lat', 'lon')
Inputs may be any that keep to these rules, and one draw needn't show every extreme that they name: `var_ids`: each variable number appears once.
All inputs are finite; a program needn't handle non-finite values.
Results may differ from a plain program's by a relative error of at most 0.015.
The roundings to bfloat16 on the way count: a program that leaves them out, or rounds other values in their place, can miss the bound.
Values may be sent and summed in bfloat16 or wider, within the bound.
A program may use at most 128 MiB of HBM per device.

v0:
```python
import jax
import jax.numpy as jnp
from jax import lax
from jax.sharding import PartitionSpec as P

HEADS = 16
HEAD_DIM = 64
RADIUS = 16


def from_behind(block, axis, distance):
    devices = range(lax.axis_size(axis))
    route = [((i - distance) % len(devices), i) for i in devices]
    return lax.ppermute(block, axis, route)


def variable_vectors(var_ids, var_embed):
    count = var_embed.shape[0]
    onehot = (var_ids[:, None] == jnp.arange(count, dtype=jnp.int32)[None, :]).astype(jnp.float32)
    return jnp.dot(onehot, var_embed.astype(jnp.float32), precision=lax.Precision.HIGHEST)


def embed_patches(pixel_block, patch_w, vectors):
    nvar, two_rows, two_cols = pixel_block.shape
    patches = pixel_block.reshape(nvar, two_rows // 2, 2, two_cols // 2, 2)
    patches = patches.transpose(0, 1, 3, 2, 4).reshape(nvar, two_rows // 2, two_cols // 2, 4)
    result = jnp.einsum(
        "vrck,vkd->vrcd", patches, patch_w.astype(jnp.float32), precision=lax.Precision.HIGHEST
    )
    return (result + vectors[:, None, None, :]).astype(jnp.bfloat16)


def aggregate(embedded, agg_score, agg_value, agg_out):
    nvar, row_count, col_count, width = embedded.shape
    flat = embedded.reshape(nvar, row_count * col_count, width)
    scores = jnp.einsum("vtd,dh->vth", flat, agg_score, preferred_element_type=jnp.float32)
    weights = jax.nn.softmax(scores, axis=0).astype(jnp.bfloat16)
    mixture = jnp.einsum("vth,vtd->thd", weights, flat, preferred_element_type=jnp.float32).astype(
        jnp.bfloat16
    )
    value_heads = agg_value.reshape(width, HEADS, HEAD_DIM)
    head_out = jnp.einsum(
        "thd,dhe->the", mixture, value_heads, preferred_element_type=jnp.float32
    ).astype(jnp.bfloat16)
    head_out = head_out.reshape(row_count * col_count, width)
    return jnp.dot(head_out, agg_out, preferred_element_type=jnp.float32).reshape(
        row_count, col_count, width
    )


def layer_norm(tokens, norm_gain):
    center = tokens - jnp.mean(tokens, axis=-1, keepdims=True)
    spread = jnp.mean(center * center, axis=-1, keepdims=True)
    return (center * lax.rsqrt(spread + 1e-05) * norm_gain).astype(jnp.bfloat16)


def attend(queries, key_block, value_block, window_off, col_dev):
    width = queries.shape[-1]
    head_count = window_off.shape[0]
    query_heads = queries.reshape(-1, head_count, HEAD_DIM)
    key_heads = key_block.reshape(-1, head_count, HEAD_DIM)
    value_heads = value_block.reshape(-1, head_count, HEAD_DIM)
    logits = jnp.einsum("qhe,khe->hqk", query_heads, key_heads, preferred_element_type=jnp.float32)
    logits = logits / jnp.sqrt(jnp.float32(HEAD_DIM))
    query_col = jnp.arange(query_heads.shape[0], dtype=jnp.int32) % col_dev
    key_col = jnp.arange(key_heads.shape[0], dtype=jnp.int32) % (3 * col_dev)
    col_gap = key_col[None, :] - col_dev - query_col[:, None]
    allowed = jnp.abs(col_gap[None, :, :] - window_off[:, None, None]) <= RADIUS
    logits = jnp.where(allowed, logits, jnp.float32(-1e30))
    weights = jax.nn.softmax(logits, axis=-1).astype(jnp.bfloat16)
    result = jnp.einsum("hqk,khe->qhe", weights, value_heads, preferred_element_type=jnp.float32)
    return result.astype(jnp.bfloat16).reshape(-1, width)


def per_device(
    pixels,
    patch_w,
    var_embed,
    var_ids,
    agg_score,
    agg_value,
    agg_out,
    pos_embed,
    norm_gain,
    w_query,
    w_key,
    w_value,
    w_proj,
    window_off,
):
    lon_index = lax.axis_index("lon")
    var_dev = patch_w.shape[0]
    vectors = variable_vectors(var_ids, var_embed)
    own_vectors = lax.dynamic_slice_in_dim(vectors, lon_index * var_dev, var_dev, 0)
    embedded = embed_patches(pixels, patch_w, own_vectors)
    mixed_tokens = aggregate(
        lax.all_to_all(embedded, "lon", split_axis=2, concat_axis=0, tiled=True),
        agg_score,
        agg_value,
        agg_out,
    )
    row_count, col_count, width = pos_embed.shape
    tokens = mixed_tokens + pos_embed.astype(jnp.float32)
    normed = layer_norm(tokens, norm_gain).reshape(row_count * col_count, width)
    queries = jnp.dot(normed, w_query, preferred_element_type=jnp.float32).astype(jnp.bfloat16)
    key_rows = jnp.dot(normed, w_key, preferred_element_type=jnp.float32).astype(jnp.bfloat16)
    value_rows = jnp.dot(normed, w_value, preferred_element_type=jnp.float32).astype(jnp.bfloat16)
    key_value = jnp.stack([key_rows, value_rows]).reshape(2, row_count, col_count, width)
    column_set = lax.all_gather(key_value, "lat", axis=1, tiled=True)
    western = from_behind(column_set, "lon", 1)
    eastern = from_behind(column_set, "lon", -1)
    window_set = jnp.concatenate([western, column_set, eastern], axis=2)
    key_block = window_set[0].reshape(-1, width)
    value_block = window_set[1].reshape(-1, width)
    all_query = jnp.concatenate([queries] * 1, axis=0)
    attended = attend(all_query, key_block, value_block, window_off, col_count)
    attended = attended.reshape(row_count, -1, col_count, width)
    attended = attended.transpose(1, 0, 2, 3)
    attended = attended.reshape(-1, width)
    result = tokens.reshape(row_count * col_count, width) + jnp.dot(
        attended, w_proj, preferred_element_type=jnp.float32
    )
    return result.astype(jnp.bfloat16).reshape(row_count, col_count, width)


def solution(mesh):
    placed = (
        P("lon", "lat", None),
        P("lon", None, None),
        P(),
        P(),
        P(),
        P(),
        P(),
        P("lat", "lon", None),
        P(),
        P(),
        P(),
        P(),
        P(),
        P(),
    )
    return jax.shard_map(
        per_device, mesh=mesh, in_specs=placed, out_specs=P("lat", "lon", None), check_vma=False
    )
```

profile of v0, /device:TPU:2, one launch (start us, length us, event | category | flops | bytes accessed | tf_op | source)
XLA Modules:
  0.0 524.5 jit_solution(15942936236662157920)
XLA Ops:
  6.5 0.0 copy-start
  6.5 7.3 %reshape.111 = f32[1,2,2,2048,2]{4,3,2,1,0:T(8,128)} reshape(f32[1,4,4096]{2,1,0:T(4,128)} %param.14) | data formatting | bytes 131072 | tf_op jit(solution)/shard_map/reshape | solution.py:25
  13.8 2.8 copy.39
  16.7 0.0 copy-done.11
  16.7 0.0 copy-done.7
  16.7 0.2 fusion.31
  16.9 0.0 copy-done.9
  16.9 7.2 %fusion.8 = bf16[1,2,2048,1024]{3,2,1,0:T(8,128)(2,1)S(1)} fusion(f32[1024]{0:T(1024)S(1)} %bitcast.81, f32[2,2048,4]{1,0,2:T(2,128)S(1)} %bitcast.78, bf16[1,4,1024]{2,1,0:T(4,128)(2,1)S(1)} %copy-done.9), kind=kOutput, calls=%fused_computation.13 | convolution fusion | flops 209715200 | bytes 8466432 | tf_op jit(solution)/shard_map/vrck,vkd->vrcd/dot_general | solution.py:27
  24.2 29.2 %copy.41 = bf16[1,2,2048,1024]{3,1,0,2:T(2,128)(2,1)} copy(bf16[1,2,2048,1024]{3,2,1,0:T(8,128)(2,1)S(1)} %fusion.8) | data formatting | bytes 16777216 | tf_op jit(solution)/shard_map/convert_element_type | solution.py:30
  53.4 10.1 %all-to-all-start = ((bf16[1,2,2048,1024]{3,1,0,2:T(2,128)(2,1)}), bf16[1,2,2048,1024]{3,1,0,2:T(2,128)(2,1)}, u32[]{:S(2)}, u32[]{:S(2)}) async-start(bf16[1,2,2048,1024]{3,1,0,2:T(2,128)(2,1)} %copy.41), calls=%async_computation | async-start | bytes 16777216 | tf_op jit(solution)/shard_map/all_to_all | solution.py:97
  63.6 0.0 all-gather.2.cloned.1.call-start
  63.6 4.4 copy.45
  68.0 180.6 %all-to-all-done = bf16[1,2,2048,1024]{3,1,0,2:T(2,128)(2,1)} async-done(((bf16[1,2,2048,1024]{3,1,0,2:T(2,128)(2,1)}), bf16[1,2,2048,1024]{3,1,0,2:T(2,128)(2,1)}, u32[]{:S(2)}, u32[]{:S(2)}) %all-to-all-start) | async-done | bytes 8388640 | tf_op jit(solution)/shard_map/all_to_all | solution.py:97
  248.6 11.3 %copy.57 = bf16[1,2,32,64,1024]{4,2,3,1,0:T(8,128)(2,1)} copy(bf16[1,2,32,64,1024]{4,1,3,2,0:T(2,128)(2,1)} %bitcast.6) | data formatting | bytes 16777216 | tf_op jit(solution)/shard_map/reshape | solution.py:35
  259.9 9.5 %copy.42 = bf16[1,2,32,64,1024]{4,3,1,2,0:T(8,128)(2,1)} copy(bf16[1,2,32,64,1024]{4,1,3,2,0:T(2,128)(2,1)} %bitcast.6) | data formatting | bytes 16777216 | tf_op jit(solution)/shard_map/all_to_all | solution.py:97
  269.4 0.0 copy-done.8
  269.4 5.7 %fusion.42 = (f32[128,16]{0,1:T(8,128)S(1)}, f32[32,128,16]{1,2,0:T(8,128)S(1)}) fusion(bf16[32,128,1024]{2,1,0:T(8,128)(2,1)} %bitcast.68, bf16[1024,16]{0,1:T(8,128)(2,1)S(1)} %copy-done.8), kind=kOutput, calls=%fused_computation.61 | convolution fusion | flops 134281216 | bytes 8691712 | tf_op jit(solution)/shard_map/vtd,dh->vth/dot_general | solution.py:36
  275.1 0.1 fusion.27
  275.2 0.1 divide_convert_fusion.4
  275.2 0.5 copy.43
  275.7 0.0 copy-start.5
  275.7 4.8 convolution_convert_fusion
  280.5 0.0 copy-start.6
  280.5 0.0 copy-done.5
  280.5 0.0 copy-start.10
  280.5 2.8 fusion.23
  283.3 0.2 reshape.123
  283.6 0.0 copy-done
  283.6 0.0 copy-done.6
  283.6 0.0 copy-start.3
  283.6 0.6 fusion.43
  284.2 0.2 multiply_reduce_fusion
  284.4 0.0 copy-done.10
  284.4 0.1 multiply_convert_fusion
  284.6 2.0 convolution_convert_fusion.2
  286.6 0.0 copy-done.3
  286.6 0.4 convolution_convert_fusion.3
  287.1 0.8 pad_maximum_fusion
  287.9 0.0 all-gather.2.cloned.1.call-update
  287.9 77.6 %all-gather.2.cloned.1.call-done = bf16[2,16,64,1024]{3,2,0,1:T(8,128)(2,1)} async-done(((bf16[2,2,64,1024]{3,2,0,1:T(8,128)(2,1)}), bf16[2,16,64,1024]{3,2,0,1:T(8,128)(2,1)}) %all-gather.2.cloned.1.call-update) | async-done | bytes 4194320 | tf_op jit(solution)/shard_map/all_gather | solution.py:109
  365.5 4.9 copy.50
  370.4 0.0 collective-permute-start
  370.4 3.9 collective-permute-start.1
  374.3 0.2 broadcast_subtract_fusion
  374.5 2.0 convolution_convert_fusion.1
  376.5 0.2 copy.55
  376.7 0.0 copy-start.2
  376.7 44.0 %collective-permute-done = bf16[2,16,64,1024]{3,2,1,0:T(8,128)(2,1)} collective-permute-done((bf16[2,16,64,1024]{3,2,1,0:T(8,128)(2,1)}, bf16[2,16,64,1024]{3,2,1,0:T(8,128)(2,1)}, u32[]{:S(2)}, u32[]{:S(2)}) %collective-permute-start) | collective-permute-done | bytes 4194336 | tf_op jit(solution)/shard_map/ppermute | solution.py:14
  420.7 2.6 copy_dynamic-update-slice_fusion.1
  423.4 0.0 copy-done.2
  423.4 0.7 constant_dynamic-update-slice_fusion
  424.1 0.0 collective-permute-done.1
  424.1 2.6 copy_dynamic-update-slice_fusion
  426.7 5.2 fusion.41
  432.0 12.6 %copy.56 = bf16[1,16,192,1024]{2,1,3,0:T(8,128)(2,1)} copy(bf16[1,16,192,1024]{3,2,0,1:T(8,128)(2,1)} %get-tuple-element.5) | data formatting | bytes 12582912 | tf_op jit(solution)/shard_map/slice | solution.py:113
  444.6 14.0 %reshape_reshape_squeeze.7 = bf16[3072,16,64]{0,2,1:T(8,128)(2,1)} reshape(bf16[1,16,192,1024]{2,1,3,0:T(8,128)(2,1)} %copy.56) | data formatting | bytes 12582912 | tf_op jit(solution)/shard_map/reshape;reshape;squeeze | solution.py:61
  458.6 12.6 %copy.54 = bf16[1,16,192,1024]{2,1,3,0:T(8,128)(2,1)} copy(bf16[1,16,192,1024]{3,2,0,1:T(8,128)(2,1)} %get-tuple-element.6) | data formatting | bytes 12582912 | tf_op jit(solution)/shard_map/slice | solution.py:114
  471.2 14.0 %reshape_reshape_squeeze.6 = bf16[3072,16,64]{0,2,1:T(8,128)(2,1)} reshape(bf16[1,16,192,1024]{2,1,3,0:T(8,128)(2,1)} %copy.54) | data formatting | bytes 12582912 | tf_op jit(solution)/shard_map/reshape;reshape;squeeze | solution.py:62
  485.2 0.0 copy-done.12
  485.2 18.5 %fusion.44 = (f32[16,128]{1,0:T(8,128)S(1)}, f32[16,128,3072]{2,1,0:T(8,128)}) fusion(s32[16]{0:T(128)S(1)} %copy-done.12, s32[128,3072]{1,0:T(8,128)S(1)} %broadcast_subtract_fusion, bf16[128,16,64]{0,2,1:T(8,128)(2,1)S(1)} %bitcast.80, bf16[3072,16,64]{0,2,1:T(8,128)(2,1)} %reshape_reshape_squeeze.7), kind=kOutput, calls=%fused_computation.63 | convolution fusion | flops 849349632 | bytes 33300544 | tf_op jit(solution)/shard_map/sub | solution.py:70
  503.7 12.6 %fusion.18 = bf16[16,64,128]{2,1,0:T(8,128)(2,1)S(1)} fusion(bf16[3072,16,64]{0,2,1:T(8,128)(2,1)} %reshape_reshape_squeeze.6, f32[16,128,3072]{2,1,0:T(8,128)} %get-tuple-element.12, f32[16,128]{1,0:T(8,128)S(1)} %get-tuple-element.11), kind=kOutput, calls=%fused_computation.24 | convolution fusion | flops 818020352 | bytes 31727616 | tf_op jit(solution)/shard_map/hqk,khe->qhe/dot_general | solution.py:71
  516.3 0.0 copy-done.4
  516.3 1.2 fusion.22
  517.5 0.0 copy-done.1
  (12 shorter events, 0.1 us)
Async XLA Ops:
  6.5 277.1 %copy-start = (bf16[1024,1024]{1,0:T(8,128)(2,1)S(1)}, bf16[1024,1024]{1,0:T(8,128)(2,1)}, u32[]{:S(2)}) copy-start(bf16[1024,1024]{1,0:T(8,128)(2,1)} %param.20) | copy-start | bytes 6291460
  6.5 10.1 %copy-start.11 = (s32[32]{0:T(128)S(1)}, s32[32]{0:T(128)}, u32[]{:S(2)}) copy-start(s32[32]{0:T(128)} %param.17) | copy-start | bytes 388
  6.5 10.1 %copy-start.7 = (bf16[32,1024]{1,0:T(8,128)(2,1)S(1)}, bf16[32,1024]{1,0:T(8,128)(2,1)}, u32[]{:S(2)}) copy-start(bf16[32,1024]{1,0:T(8,128)(2,1)} %param.16) | copy-start | bytes 196612
  6.5 10.4 %copy-start.9 = (bf16[1,4,1024]{2,1,0:T(4,128)(2,1)S(1)}, bf16[1,4,1024]{2,1,0:T(4,128)(2,1)}, u32[]{:S(2)}) copy-start(bf16[1,4,1024]{2,1,0:T(4,128)(2,1)} %param.15) | copy-start | bytes 24580
  53.4 195.2 %all-to-all-start = ((bf16[1,2,2048,1024]{3,1,0,2:T(2,128)(2,1)}), bf16[1,2,2048,1024]{3,1,0,2:T(2,128)(2,1)}, u32[]{:S(2)}, u32[]{:S(2)}) async-start(bf16[1,2,2048,1024]{3,1,0,2:T(2,128)(2,1)} %copy.41), calls=%async_computation | async-start | bytes 16777216 | tf_op jit(solution)/shard_map/all_to_all | solution.py:97
  63.6 302.0 %all-gather.2.cloned.1.call-start = ((), (), s32[]{:S(2)}) async-start(), calls=%async_computation.1 | async-start | bytes 4718592 | tf_op jit(solution)/shard_map/all_gather | solution.py:109
  259.9 9.5 %copy-start.8 = (bf16[1024,16]{0,1:T(8,128)(2,1)S(1)}, bf16[1024,16]{0,1:T(8,128)(2,1)}, u32[]{:S(2)}) copy-start(bf16[1024,16]{0,1:T(8,128)(2,1)} %param.18) | copy-start | bytes 98308
  275.7 4.8 copy-start.5
  280.5 3.1 copy-start.6
  280.5 3.9 copy-start.10
  283.6 3.0 copy-start.3
  370.4 50.4 %collective-permute-start = (bf16[2,16,64,1024]{3,2,1,0:T(8,128)(2,1)}, bf16[2,16,64,1024]{3,2,1,0:T(8,128)(2,1)}, u32[]{:S(2)}, u32[]{:S(2)}) collective-permute-start(bf16[2,16,64,1024]{3,2,1,0:T(8,128)(2,1)} %copy.50), channel_id=1, source_target_pairs={{248,0},{0,8},{8,16},{16,24},{24,32},{32,40},{40,48},{48,56},{56,6... | collective-permute-start | bytes 12582920 | tf_op jit(solution)/shard_map/ppermute | solution.py:14
  370.4 53.7 %collective-permute-start.1 = (bf16[2,16,64,1024]{3,2,1,0:T(8,128)(2,1)}, bf16[2,16,64,1024]{3,2,1,0:T(8,128)(2,1)}, u32[]{:S(2)}, u32[]{:S(2)}) collective-permute-start(bf16[2,16,64,1024]{3,2,1,0:T(8,128)(2,1)} %copy.50), channel_id=1, source_target_pairs={{8,0},{16,8},{24,16},{32,24},{40,32},{48,40},{56,48},{64,56},{72,6... | collective-permute-start | bytes 12582920 | tf_op jit(solution)/shard_map/ppermute | solution.py:14
  376.7 46.7 %copy-start.2 = (bf16[2,16,64,1024]{3,2,0,1:T(8,128)(2,1)S(1)}, bf16[2,16,64,1024]{3,2,0,1:T(8,128)(2,1)}, u32[]{:S(2)}) copy-start(bf16[2,16,64,1024]{3,2,0,1:T(8,128)(2,1)} %all-gather.2.cloned.1.call-done) | copy-start | bytes 12582916
  471.2 14.0 %copy-start.12 = (s32[16]{0:T(128)S(1)}, s32[16]{0:T(128)}, u32[]{:S(2)}) copy-start(s32[16]{0:T(128)} %param.27) | copy-start | bytes 196
  503.7 12.6 %copy-start.4 = (bf16[1024,1024]{1,0:T(8,128)(2,1)S(1)}, bf16[1024,1024]{1,0:T(8,128)(2,1)}, u32[]{:S(2)}) copy-start(bf16[1024,1024]{1,0:T(8,128)(2,1)} %param.26) | copy-start | bytes 6291460
  503.7 13.8 %copy-start.1 = (bf16[1024,1024]{1,0:T(8,128)(2,1)S(1)}, bf16[1024,1024]{1,0:T(8,128)(2,1)}, u32[]{:S(2)}) copy-start(bf16[1024,1024]{1,0:T(8,128)(2,1)} %param.20) | copy-start | bytes 6291460
Sparse Core Ops, SparseCore 0:
  288.1 77.4 all-gather.1
where the time goes:
time: 533 us; the launch traced here: 525 us
  waiting for transfers between devices  302 us (57%)
  local copies, waits for them, and re-layouts  135 us (25%)
  matrix products  58 us (11%)
  starting transfers between devices  14 us (3%)
  between operations  13.9 us (3%)
    all_to_all x1, waiting for transfers between devices, per_device(): lax.all_to_all(embedded, 'lon', split_axis=2, concat_axis=0, tiled=True)  181 us
    all_gather x1, waiting for transfers between devices, per_device(): column_set = lax.all_gather(key_value, 'lat', axis=1, tiled=True)  77.6 us
    ppermute x2, waiting for transfers between devices, from_behind(): return lax.ppermute(block, axis, route)  44 us
    convert_element_type x1, local copies, waits for them, and re-layouts, embed_patches(): return (result + vectors[:, None, None, :]).astype(jnp.bfloat16)  29.2 us
    sub x1, matrix products, attend(): weights = jax.nn.softmax(logits, axis=-1).astype(jnp.bfloat16)  18.5 us
    slice x2, local copies, waits for them, and re-layouts, per_device(): key_block = window_set[0].reshape(-1, width)  17.9 us
    another operation x1, local copies, waits for them, and re-layouts, attend(): value_heads = value_block.reshape(-1, head_count, HEAD_DIM)  14 us
    another operation x1, local copies, waits for them, and re-layouts, attend(): key_heads = key_block.reshape(-1, head_count, HEAD_DIM)  14 us
  transfers between devices with their start and end apart: 4, of which 3 were waited for; matrix products, arithmetic and copies ran while one was open for 2% of the time, Pallas kernels for 0%

commit v1 on v0

v1 whole, which is shorter than its diff:
```python
import functools
import jax
import jax.numpy as jnp
from jax import lax
from jax.experimental import pallas as pl
from jax.experimental.pallas import tpu as pltpu
from jax.sharding import PartitionSpec as P

HEADS = 16
HEAD_DIM = 64
RADIUS = 16
OFF_MAX = 32
HALO = RADIUS + OFF_MAX
VARS = 32
WIDTH = 1024
COLS = 64
FRAME = COLS + 2 * HALO
LON = 32
LAT = 8
LANES = 128
GROUP = 16
SPAN = 64
SHIFTED = COLS - GROUP + SPAN
MASKED = -1e30
F32 = jnp.float32
BF16 = jnp.bfloat16
MESH = pl.DeviceIdType.MESH


def iota(shape, dim):
    return lax.broadcasted_iota(jnp.int32, shape, dim)


def dot(a, b):
    return jnp.dot(a, b, preferred_element_type=F32)


def dot_nt(a, b):
    return lax.dot_general(a, b, (((1,), (1,)), ((), ())), preferred_element_type=F32)


def dot_tn(a, b):
    return lax.dot_general(a, b, (((0,), (0,)), ((), ())), preferred_element_type=F32)


def roll(x, shift):
    return pltpu.roll(x, shift, 1)


def make_constants(sel, vmask, tmask):
    source = iota((256, 256), 0)
    target = (
        (source % 4) // 2 * LANES
        + (source % LANES) // 4 * 4
        + source % 2 * 2
        + source // LANES
    )
    sel[...] = (iota((256, 256), 1) == target).astype(F32).astype(BF16)
    lane = iota((256, 256), 1)
    slot = iota((256, 256), 0) // GROUP
    mine = jnp.where(lane < 192, (lane % 64) // 4, jnp.where(lane < 208, lane - 192, -1))
    vmask[...] = (mine == slot).astype(F32).astype(BF16)
    tmask[...] = (iota((GROUP, 512), 1) % GROUP == iota((GROUP, 512), 0)).astype(F32)


def variable_rows(ids, var_embed, vectors):
    onehot = (iota((VARS, VARS), 0) == ids[...]).astype(F32).astype(BF16)
    vectors[...] = dot_tn(onehot, var_embed[...]).astype(BF16)


def embedding_weights(pw_all, vectors, wflat, wk):
    for v in range(VARS):
        wflat[4 * v : 4 * v + 4, :] = pw_all[v].astype(F32)
    for half in range(2):
        part = wflat[64 * half : 64 * half + 64, :].astype(BF16)
        for piece in range(3):
            wk[half, 64 * piece : 64 * piece + 64, :] = part
        wk[half, 192:208, :] = vectors[16 * half : 16 * half + 16, :]
        wk[half, 208:256, :] = jnp.zeros((48, WIDTH), BF16)


def patch_rows(pix_all, flat, turned, sel, base):
    for v in range(VARS):
        flat[4 * v : 4 * v + 4, :] = pix_all[v]
    turned[...] = flat[...].T
    points = jnp.concatenate(
        [turned[pl.ds(0, COLS, stride=2), :], turned[pl.ds(1, COLS, stride=2), :]], axis=1
    )
    pieces = []
    rest = points
    for _ in range(3):
        part = rest.astype(BF16)
        rest = rest - part.astype(F32)
        pieces.append(dot(part, sel[...]))
    lane = iota((COLS, LANES), 1)
    low = lane < 64
    ones = ((lane >= 64) & (lane < 80)).astype(F32)
    for r in range(2):
        hi, mid, lo = (piece[:, r * LANES : (r + 1) * LANES] for piece in pieces)
        base[r, 0, :, :LANES] = jnp.where(low, hi, roll(mid, 64)).astype(BF16)
        base[r, 0, :, LANES:] = jnp.where(low, lo, ones).astype(BF16)
        base[r, 1, :, :LANES] = jnp.where(low, roll(hi, 64), mid).astype(BF16)
        base[r, 1, :, LANES:] = jnp.where(low, roll(lo, 64), ones).astype(BF16)


def over_variables(x, op):
    parts = [x[:, LANES * i : LANES * (i + 1)] for i in range(4)]
    total = op(op(parts[0], parts[1]), op(parts[2], parts[3]))
    for shift in (16, 32, 64):
        total = op(total, roll(total, shift))
    return jnp.concatenate([total] * 4, axis=1)


def aggregate_group(r, g, base, vmask, tmask, wk, score_t, embedded, mixture):
    rows = pl.ds(pl.multiple_of(g * GROUP, GROUP), GROUP)
    for half in range(2):
        points = base[r, half, rows, :]
        spread = jnp.concatenate([points] * 16, axis=0) * vmask[...]
        embedded[256 * half : 256 * half + 256, :] = dot(spread, wk[half]).astype(BF16)
    scores = dot_nt(score_t[...], embedded[...])
    power = jnp.exp(scores - over_variables(scores, jnp.maximum))
    weights = (power / over_variables(power, jnp.add)).astype(BF16).astype(F32)
    blocks = [
        jnp.broadcast_to(weights[h : h + 1, :], (GROUP, 512)) * tmask[...] for h in range(HEADS)
    ]
    blocks = jnp.concatenate(blocks, axis=0).astype(BF16)
    mixed = dot(blocks, embedded[...]).astype(BF16)
    mixture[:, rows, :] = mixed.reshape(HEADS, GROUP, WIDTH)


def head_outputs(mixture, agg_value, head_out):
    low = iota((COLS, LANES), 1) < 64
    for quad in range(4):
        rows = mixture[4 * quad : 4 * quad + 4].reshape(4 * COLS, WIDTH)
        out = dot(rows, agg_value[:, 256 * quad : 256 * quad + 256])
        for pair in range(2):
            lanes = slice(LANES * pair, LANES * (pair + 1))
            first = out[2 * pair * COLS : (2 * pair + 1) * COLS, lanes]
            second = out[(2 * pair + 1) * COLS : (2 * pair + 2) * COLS, lanes]
            at = 256 * quad + LANES * pair
            head_out[:, at : at + LANES] = jnp.where(low, first, second).astype(BF16)


def layer_norm(tokens, norm_gain):
    center = tokens - jnp.mean(tokens, axis=-1, keepdims=True)
    spread = jnp.mean(center * center, axis=-1, keepdims=True)
    return (center * lax.rsqrt(spread + 1e-05) * norm_gain).astype(BF16)


def window_bias(head, residual):
    other = 64 * (1 - head)
    lane = iota((SPAN, LANES), 1) - other
    gap = iota((SPAN, LANES), 0) - lane - residual
    hidden = (lane >= 0) & (lane < GROUP) & ((gap < 0) | (gap > 2 * RADIUS))
    return jnp.where(hidden, F32(MASKED), F32(0)).astype(BF16)


def shift_windows(s, step, win, shifted):
    for r in range(2):
        for part in range(2):
            rows = jnp.zeros((SHIFTED, LANES), BF16)
            for i in range(5):
                count = min(SHIFTED, FRAME - GROUP * i)
                piece = win[r, part, s, GROUP * i : GROUP * i + count, :]
                if count < SHIFTED:
                    piece = jnp.concatenate(
                        [piece, jnp.zeros((SHIFTED - count, LANES), BF16)], axis=0
                    )
                rows = jnp.where(step == i, piece, rows)
            shifted[r, part, s] = rows


def attend_block(first, biases, query_win, shifted, attended):
    cols = pl.ds(pl.multiple_of(first, GROUP), GROUP)
    span = pl.ds(pl.multiple_of(first, GROUP), SPAN)
    lane_q = iota((GROUP, LANES), 1)
    row_q = iota((GROUP, LANES), 0)
    lane_k = iota((SPAN, LANES), 1)
    outs = []
    for head in range(2):
        own_q = (lane_q < 64) if head == 0 else (lane_q >= 64)
        own_k = (lane_k < 64) if head == 0 else (lane_k >= 64)
        pick = (lane_q - 64 * (1 - head) == row_q).astype(F32).astype(BF16)
        scale = BF16(0.125)
        rows = [(r, s) for r in range(2) for s in range(LAT)]
        queries = [jnp.where(own_q, query_win[r, s, cols, :] * scale, pick) for r, s in rows]
        keys = [jnp.where(own_k, shifted[r, 0, s, span, :], biases[head]) for r, s in rows]
        values = [shifted[r, 1, s, span, :] for r, s in rows]
        logits = dot_nt(jnp.concatenate(queries, axis=0), jnp.concatenate(keys, axis=0))
        power = jnp.exp(logits - jnp.max(logits, axis=1, keepdims=True))
        weights = power * (1.0 / jnp.sum(power, axis=1, keepdims=True))
        outs.append(dot(weights.astype(BF16), jnp.concatenate(values, axis=0)))
    low = iota((256, LANES), 1) < 64
    result = jnp.where(low, outs[0], outs[1]).astype(BF16)
    for r in range(2):
        for s in range(LAT):
            at = (r * LAT + s) * GROUP
            attended[s, r, cols, :] = result[at : at + GROUP, :]


def kernel(
    pixels,
    patch_w,
    var_embed,
    ids,
    agg_score,
    agg_value,
    agg_out,
    pos_embed,
    norm_gain,
    w_query,
    w_key,
    w_value,
    w_proj,
    window_off,
    updated,
    pix_all,
    pw_all,
    ve,
    score,
    score_t,
    value_w,
    out_w,
    pos,
    query_w,
    key_w,
    val_w,
    proj_w,
    sel,
    vmask,
    tmask,
    vectors,
    wflat,
    wk,
    flat,
    turned,
    base,
    embedded,
    mixture,
    head_out,
    tokens,
    normed,
    query_own,
    kv_own,
    query_win,
    win,
    shifted,
    attended,
    attended_own,
    load_sem,
    pix_sem,
    pw_sem,
    kv_sem,
    kv_send,
    q_sem,
    q_send,
    halo_sem,
    halo_send,
    att_sem,
    att_send,
):
    lon = lax.axis_index("lon")
    lat = lax.axis_index("lat")
    loads = [
        pltpu.make_async_copy(src, dst, load_sem.at[i])
        for i, (src, dst) in enumerate(
            (
                (var_embed, ve),
                (agg_score, score),
                (agg_value, value_w),
                (agg_out, out_w),
                (pos_embed, pos),
                (w_key, key_w),
                (w_value, val_w),
                (w_query, query_w),
                (w_proj, proj_w),
            )
        )
    ]
    barrier = pltpu.get_barrier_semaphore()

    @pl.loop(1, LON)
    def _(d):
        pl.semaphore_signal(
            barrier, inc=1, device_id={"lon": lax.rem(lon + d, LON)}, device_id_type=MESH
        )

    @pl.loop(1, LAT)
    def _(d):
        pl.semaphore_signal(
            barrier, inc=1, device_id={"lat": lax.rem(lat + d, LAT)}, device_id_type=MESH
        )

    def pixel_part(to):
        return pixels.at[0, :, pl.ds(pl.multiple_of(to * LANES, LANES), LANES)]

    own_pix = pltpu.make_async_copy(pixel_part(lon), pix_all.at[lon], pix_sem.at[0])
    own_pw = pltpu.make_async_copy(patch_w.at[0], pw_all.at[lon], pw_sem.at[0])
    own_pix.start()
    own_pw.start()
    for load in loads:
        load.start()
    make_constants(sel, vmask, tmask)
    pl.semaphore_wait(barrier, LON + LAT - 2)

    @pl.loop(1, LON)
    def _(d):
        to = lax.rem(lon + d, LON)
        pltpu.make_async_remote_copy(
            src_ref=pixel_part(to),
            dst_ref=pix_all.at[lon],
            send_sem=pix_sem.at[1],
            recv_sem=pix_sem.at[0],
            device_id={"lon": to},
            device_id_type=MESH,
        ).start()
        pltpu.make_async_remote_copy(
            src_ref=patch_w.at[0],
            dst_ref=pw_all.at[lon],
            send_sem=pw_sem.at[1],
            recv_sem=pw_sem.at[0],
            device_id={"lon": to},
            device_id_type=MESH,
        ).start()

    loads[0].wait()
    variable_rows(ids, ve, vectors)
    loads[1].wait()
    identity = (iota((HEADS, HEADS), 0) == iota((HEADS, HEADS), 1)).astype(F32).astype(BF16)
    score_t[...] = dot_nt(identity, score[...]).astype(BF16)

    def wait_bytes(ref, sem):
        pltpu.make_async_copy(ref, ref, sem).wait()

    wait_bytes(pix_all, pix_sem.at[0])
    patch_rows(pix_all, flat, turned, sel, base)
    wait_bytes(pw_all, pw_sem.at[0])
    embedding_weights(pw_all, vectors, wflat, wk)

    def lanes_of(device):
        return pl.ds(pl.multiple_of(device * LANES, LANES), LANES)

    def kv_part(r, to):
        return kv_own.at[r, :, :, lanes_of(to)]

    def kv_place(r, s):
        return win.at[r, :, s, pl.ds(HALO, COLS), :]

    def send_to_all(part, place, send_sem, recv_sem):
        own = pltpu.make_async_copy(part(lat), place(lat), recv_sem)
        own.start()

        @pl.loop(1, LAT)
        def _(d):
            to = lax.rem(lat + d, LAT)
            pltpu.make_async_remote_copy(
                src_ref=part(to),
                dst_ref=place(lat),
                send_sem=send_sem,
                recv_sem=recv_sem,
                device_id={"lat": to},
                device_id_type=MESH,
            ).start()

    east_of = lax.rem(lon + 1, LON)
    west_of = lax.rem(lon + LON - 1, LON)

    def send_halos(r):
        @pl.loop(0, LAT)
        def _(d):
            s = lax.rem(lat + LAT - d, LAT)
            wait_bytes(kv_place(r, s), kv_sem.at[r, s])
            pltpu.make_async_remote_copy(
                src_ref=win.at[r, :, s, pl.ds(HALO + COLS - HALO, HALO), :],
                dst_ref=win.at[r, :, s, pl.ds(0, HALO), :],
                send_sem=halo_send.at[r, 0],
                recv_sem=halo_sem.at[r, 0],
                device_id={"lon": east_of},
                device_id_type=MESH,
            ).start()
            pltpu.make_async_remote_copy(
                src_ref=win.at[r, :, s, pl.ds(HALO, HALO), :],
                dst_ref=win.at[r, :, s, pl.ds(HALO + COLS, HALO), :],
                send_sem=halo_send.at[r, 1],
                recv_sem=halo_sem.at[r, 1],
                device_id={"lon": west_of},
                device_id_type=MESH,
            ).start()

    for r in range(2):

        @pl.loop(0, COLS // GROUP)
        def _(g):
            aggregate_group(r, g, base, vmask, tmask, wk, score_t, embedded, mixture)

        if r == 0:
            loads[2].wait()
        head_outputs(mixture, value_w, head_out)
        if r == 0:
            loads[3].wait()
            loads[4].wait()
        tokens[r] = dot(head_out[...], out_w[...]) + pos[r].astype(F32)
        normed[...] = layer_norm(tokens[r], norm_gain[...])
        if r == 0:
            loads[5].wait()
            loads[6].wait()
        kv_own[r, 0] = dot(normed[...], key_w[...]).astype(BF16)
        kv_own[r, 1] = dot(normed[...], val_w[...]).astype(BF16)
        own = pltpu.make_async_copy(kv_part(r, lat), kv_place(r, lat), kv_sem.at[r, lat])
        own.start()

        @pl.loop(1, LAT)
        def _(d):
            to = lax.rem(lat + d, LAT)
            pltpu.make_async_remote_copy(
                src_ref=kv_part(r, to),
                dst_ref=kv_place(r, lat),
                send_sem=kv_send.at[r],
                recv_sem=kv_sem.at[r, lat],
                device_id={"lat": to},
                device_id_type=MESH,
            ).start()

        if r == 0:
            loads[7].wait()
        query_own[r] = dot(normed[...], query_w[...]).astype(BF16)
        send_to_all(
            lambda to: query_own.at[r, :, lanes_of(to)],
            lambda s: query_win.at[r, s],
            q_send.at[r],
            q_sem.at[r],
        )
        if r == 1:
            send_halos(0)
            send_halos(1)

    for r in range(2):
        wait_bytes(query_win.at[r], q_sem.at[r])
        for side in range(2):
            wait_bytes(win.at[r, :, :, pl.ds(0, HALO), :], halo_sem.at[r, side])

    shifts = [window_off[2 * lat + head] + OFF_MAX for head in range(2)]
    step = jnp.where(iota((SHIFTED, LANES), 1) < 64, shifts[0], shifts[1]) >> 4
    biases = [window_bias(head, shifts[head] & (GROUP - 1)) for head in range(2)]

    @pl.loop(0, LAT)
    def _(s):
        shift_windows(s, step, win, shifted)

    for half in range(2):

        @pl.loop(0, 2)
        def _(block):
            attend_block((2 * half + block) * GROUP, biases, query_win, shifted, attended)

        cols = pl.ds(32 * half, 32)
        send_to_all(
            lambda to: attended.at[to, :, cols, :],
            lambda s: attended_own.at[:, cols, lanes_of(s)],
            att_send.at[half],
            att_sem.at[half],
        )
    loads[8].wait()
    for half in range(2):
        wait_bytes(attended_own.at[:, pl.ds(32 * half, 32), :], att_sem.at[half])
    rows = attended_own[...].reshape(2 * COLS, WIDTH)
    result = tokens[...].reshape(2 * COLS, WIDTH) + dot(rows, proj_w[...])
    updated[...] = result.astype(BF16).reshape(2, COLS, WIDTH)

    wait_bytes(pix_all.at[pl.ds(0, LON - 1)], pix_sem.at[1])
    wait_bytes(pw_all.at[pl.ds(0, LON - 1)], pw_sem.at[1])
    for r in range(2):
        wait_bytes(win.at[r, :, pl.ds(0, LAT - 1), pl.ds(0, COLS), :], kv_send.at[r])
        wait_bytes(query_win.at[r, pl.ds(0, LAT - 1)], q_send.at[r])
        for side in range(2):
            wait_bytes(win.at[r, :, :, pl.ds(0, HALO), :], halo_send.at[r, side])
        wait_bytes(attended.at[pl.ds(0, LAT - 1), :, pl.ds(0, 32), :], att_send.at[r])


def per_device(
    pixels,
    patch_w,
    var_embed,
    var_ids,
    agg_score,
    agg_value,
    agg_out,
    pos_embed,
    norm_gain,
    w_query,
    w_key,
    w_value,
    w_proj,
    window_off,
):
    hbm = pl.BlockSpec(memory_space=pl.ANY)
    vmem = pl.BlockSpec(memory_space=pltpu.VMEM)
    smem = pl.BlockSpec(memory_space=pltpu.SMEM)
    square = pltpu.VMEM((WIDTH, WIDTH), BF16)
    dma = pltpu.SemaphoreType.DMA
    scratch = [
        pltpu.VMEM((VARS, 4, LANES), F32),
        pltpu.VMEM((VARS, 4, WIDTH), BF16),
        pltpu.VMEM((VARS, WIDTH), BF16),
        pltpu.VMEM((WIDTH, HEADS), BF16),
        pltpu.VMEM((HEADS, WIDTH), BF16),
        square,
        square,
        pltpu.VMEM((2, COLS, WIDTH), BF16),
        square,
        square,
        square,
        square,
        pltpu.VMEM((256, 256), BF16),
        pltpu.VMEM((256, 256), BF16),
        pltpu.VMEM((GROUP, 512), F32),
        pltpu.VMEM((VARS, WIDTH), BF16),
        pltpu.VMEM((4 * VARS, WIDTH), F32),
        pltpu.VMEM((2, 256, WIDTH), BF16),
        pltpu.VMEM((4 * VARS, LANES), F32),
        pltpu.VMEM((LANES, 4 * VARS), F32),
        pltpu.VMEM((2, 2, COLS, 256), BF16),
        pltpu.VMEM((512, WIDTH), BF16),
        pltpu.VMEM((HEADS, COLS, WIDTH), BF16),
        pltpu.VMEM((COLS, WIDTH), BF16),
        pltpu.VMEM((2, COLS, WIDTH), F32),
        pltpu.VMEM((COLS, WIDTH), BF16),
        pltpu.VMEM((2, COLS, WIDTH), BF16),
        pltpu.VMEM((2, 2, COLS, WIDTH), BF16),
        pltpu.VMEM((2, LAT, COLS, LANES), BF16),
        pltpu.VMEM((2, 2, LAT, FRAME, LANES), BF16),
        pltpu.VMEM((2, 2, LAT, SHIFTED, LANES), BF16),
        pltpu.VMEM((LAT, 2, COLS, LANES), BF16),
        pltpu.VMEM((2, COLS, WIDTH), BF16),
        dma((9,)),
        dma((2,)),
        dma((2,)),
        dma((2, LAT)),
        dma((2,)),
        dma((2,)),
        dma((2,)),
        dma((2, 2)),
        dma((2, 2)),
        dma((2,)),
        dma((2,)),
    ]
    return pl.pallas_call(
        kernel,
        out_shape=jax.ShapeDtypeStruct((2, COLS, WIDTH), BF16),
        in_specs=[hbm, hbm, hbm, vmem, hbm, hbm, hbm, hbm, vmem, hbm, hbm, hbm, hbm, smem],
        out_specs=vmem,
        scratch_shapes=scratch,
        compiler_params=pltpu.CompilerParams(
            collective_id=0, has_side_effects=True, vmem_limit_bytes=48 * 1024 * 1024
        ),
        name="weather_step",
    )(
        pixels,
        patch_w,
        var_embed,
        var_ids.reshape(1, VARS),
        agg_score,
        agg_value,
        agg_out,
        pos_embed,
        norm_gain.reshape(1, WIDTH),
        w_query,
        w_key,
        w_value,
        w_proj,
        window_off,
    )


def solution(mesh):
    placed = (
        P("lon", "lat", None),
        P("lon", None, None),
        P(),
        P(),
        P(),
        P(),
        P(),
        P("lat", "lon", None),
        P(),
        P(),
        P(),
        P(),
        P(),
        P(),
    )
    return jax.shard_map(
        per_device, mesh=mesh, in_specs=placed, out_specs=P("lat", "lon", None), check_vma=False
    )
```

time: 533 us -> 72.6 us (0.14); the launches traced: 525 us -> 71.7 us
  waiting for transfers between devices: 302 us -> 0 us
  local copies, waits for them, and re-layouts: 135 us -> 10.1 us
  Pallas kernels: 0 us -> 61.6 us
  matrix products: 58 us -> 0 us
  starting transfers between devices: 14 us -> 0 us
  between operations: 13.9 us -> 0.03 us
    all_to_all x1 -> x0, waiting for transfers between devices: 181 us -> none  [per_device(): lax.all_to_all(embedded, 'lon', split_axis=2, concat_axis=0, tiled=True)]
    all_gather x1 -> x0, waiting for transfers between devices: 77.6 us -> none  [per_device(): column_set = lax.all_gather(key_value, 'lat', axis=1, tiled=True)]
    pallas_call x0 -> x1, Pallas kernels: none -> 61.6 us  [per_device(): pl.pallas_call(kernel, out_shape=jax.ShapeDtypeStruct((2, COLS, WIDTH), B...]
    ppermute x2 -> x0, waiting for transfers between devices: 44 us -> none  [from_behind(): return lax.ppermute(block, axis, route)]
    dot_general x11 -> x0, matrix products: 39.5 us -> none  [the longest x1 12.6 us: attend(): jnp.einsum('hqk,khe->qhe', weights, value_heads, preferred_element_type=j...]
    slice x3 -> x0, local copies, waits for them, and re-layouts: 30.5 us -> none  [the longest x2 17.9 us: per_device(): key_block = window_set[0].reshape(-1, width)]
    convert_element_type x3 -> x0, local copies, waits for them, and re-layouts: 29.9 us -> none  [the longest x1 29.2 us: embed_patches(): return (result + vectors[:, None, None, :]).astype(jnp.bfloat16)]
    another operation x2 -> x0, local copies, waits for them, and re-layouts: 28 us -> none  [the longest x1 14 us: attend(): value_heads = value_block.reshape(-1, head_count, HEAD_DIM)]
  transfers between devices with their start and end apart: 4 -> 0, of which waited for: 3 -> 0; matrix products, arithmetic and copies ran while one was open for 2% -> 0% of each run, Pallas kernels for 0% -> 0%
where the time goes in v1:
time: 72.6 us; the launch traced here: 71.7 us
  Pallas kernels  61.6 us (85%)
  local copies, waits for them, and re-layouts  10.1 us (14%)
    pallas_call x1, Pallas kernels, per_device(): pl.pallas_call(kernel, out_shape=jax.ShapeDtypeStruct((2, COLS, WIDTH), B...  61.6 us
    unnamed x20, local copies, waits for them, and re-layouts  10.1 us

profile of v1, /device:TPU:2, one launch (start us, length us, event | category | flops | bytes accessed | tf_op | source)
XLA Modules:
  0.0 71.7 jit_solution(14985542044031190473)
XLA Ops:
  0.0 0.9 %copy.15.agg_score = bf16[1024,16]{1,0:T(8,128)(2,1)S(1)} copy(bf16[1024,16]{0,1:T(8,128)(2,1)} %param.18) | data formatting | bytes 65536 | tf_op args[4]
  0.9 0.0 copy-start
  0.9 1.6 %copy-done = bf16[1024,1024]{1,0:T(8,128)(2,1)S(1)} copy-done((bf16[1024,1024]{1,0:T(8,128)(2,1)S(1)}, bf16[1024,1024]{1,0:T(8,128)(2,1)}, u32[]{:S(2)}) %copy-start) | copy-done | bytes 2097176
  2.5 0.0 copy-start.1
  2.5 1.6 %copy-done.1 = bf16[1024,1024]{1,0:T(8,128)(2,1)S(1)} copy-done((bf16[1024,1024]{1,0:T(8,128)(2,1)S(1)}, bf16[1024,1024]{1,0:T(8,128)(2,1)}, u32[]{:S(2)}) %copy-start.1) | copy-done | bytes 2097176
  4.1 0.0 copy-start.2
  4.1 0.9 %copy-done.2 = bf16[2,64,1024]{2,1,0:T(8,128)(2,1)S(1)} copy-done((bf16[2,64,1024]{2,1,0:T(8,128)(2,1)S(1)}, bf16[2,64,1024]{2,1,0:T(8,128)(2,1)}, u32[]{:S(2)}) %copy-start.2) | copy-done | bytes 262168
  5.1 0.0 copy-start.3
  5.1 0.8 %copy-done.3 = f32[1,4,4096]{2,1,0:T(4,128)S(1)} copy-done((f32[1,4,4096]{2,1,0:T(4,128)S(1)}, f32[1,4,4096]{2,1,0:T(4,128)}, u32[]{:S(2)}) %copy-start.3) | copy-done | bytes 65560
  5.9 0.0 copy-start.4
  5.9 0.8 %copy-done.4 = bf16[32,1024]{1,0:T(8,128)(2,1)S(1)} copy-done((bf16[32,1024]{1,0:T(8,128)(2,1)S(1)}, bf16[32,1024]{1,0:T(8,128)(2,1)}, u32[]{:S(2)}) %copy-start.4) | copy-done | bytes 65560
  6.8 0.0 copy-start.5
  6.8 0.7 copy-done.5
  7.4 0.0 copy-start.6
  7.5 0.7 copy-done.6
  8.1 0.0 copy-start.7
  8.1 0.7 copy-done.7
  8.8 0.0 copy-start.8
  8.8 0.7 copy-done.8
  9.4 61.6 %weather_step.1 = bf16[2,64,1024]{2,1,0:T(8,128)(2,1)S(1)} custom-call(f32[1,4,4096]{2,1,0:T(4,128)S(1)} %copy-done.3, bf16[1,4,1024]{2,1,0:T(4,128)(2,1)S(1)} %copy-done.5, bf16[32,1024]{1,0:T(8,128)(2,1)S(1)} %copy-done.4, s32[1,32]{1,0:T(1,128)S(1)} %bitcast.3, bf16[1024,16]{1,0:T(8,128)(2,1)S(1)} %copy.15.agg_score, bf16[1024,1024]{1,0:T(8,128)(2,1)S(1)} %copy-done, ...), custom_call_target="tpu_custom_call" | custom-call | tf_op jit(solution)/shard_map/weather_step/pallas_call | solution.py:547
  71.0 0.7 copy.17
Async XLA Ops:
  0.9 1.6 %copy-start = (bf16[1024,1024]{1,0:T(8,128)(2,1)S(1)}, bf16[1024,1024]{1,0:T(8,128)(2,1)}, u32[]{:S(2)}) copy-start(bf16[1024,1024]{1,0:T(8,128)(2,1)} %agg_value.1) | copy-start | bytes 6291460
  2.5 1.6 %copy-start.1 = (bf16[1024,1024]{1,0:T(8,128)(2,1)S(1)}, bf16[1024,1024]{1,0:T(8,128)(2,1)}, u32[]{:S(2)}) copy-start(bf16[1024,1024]{1,0:T(8,128)(2,1)} %agg_out.1) | copy-start | bytes 6291460
  4.1 0.9 %copy-start.2 = (bf16[2,64,1024]{2,1,0:T(8,128)(2,1)S(1)}, bf16[2,64,1024]{2,1,0:T(8,128)(2,1)}, u32[]{:S(2)}) copy-start(bf16[2,64,1024]{2,1,0:T(8,128)(2,1)} %pos_embed.1) | copy-start | bytes 786436
  5.1 0.8 %copy-start.3 = (f32[1,4,4096]{2,1,0:T(4,128)S(1)}, f32[1,4,4096]{2,1,0:T(4,128)}, u32[]{:S(2)}) copy-start(f32[1,4,4096]{2,1,0:T(4,128)} %pixels.1) | copy-start | bytes 196612
  5.9 0.8 %copy-start.4 = (bf16[32,1024]{1,0:T(8,128)(2,1)S(1)}, bf16[32,1024]{1,0:T(8,128)(2,1)}, u32[]{:S(2)}) copy-start(bf16[32,1024]{1,0:T(8,128)(2,1)} %var_embed.1) | copy-start | bytes 196612
  6.8 0.7 copy-start.5
  7.4 0.7 copy-start.6
  8.1 0.7 copy-start.7
  8.8 0.7 copy-start.8
